TPU v7x, 32 devices: a whole 2x2x4 slice. The times are simulated.
32 devices in a mesh: dev: 32 (over z, y, x, core).
Axes of the slice: x: 2, y: 2, z: 4, core: 2. Of those that a mesh axis runs over, the one named last changes fastest.
Arguments:
- log_depth: float32 [256, 12544], P('dev'), may hold values from -1.5 to 1.5
- depth_m: float32 [256, 12544], P('dev'), may hold values from -0.006 to 0.006
- depth_v: float32 [256, 12544], P('dev'), may hold values from 1e-07 to 1e-05
- image_params: float32 [7, 256], P(None, 'dev'), may hold values from -1.5 to 1.5
- image_m: float32 [7, 256], P(None, 'dev'), may hold values from -6 to 6
- image_v: float32 [7, 256], P(None, 'dev'), may hold values from 0.1 to 10
- pair_points: bfloat16 [768, 2, 3, 12544], P('dev'), may hold values from -6 to 6
- pair_conf: bfloat16 [768, 2, 12544], P('dev'), may hold values from 1 to 5
- pair_params: float32 [7, 768], P(None, 'dev'), may hold values from -1.5 to 1.5
- pair_m: float32 [7, 768], P(None, 'dev'), may hold values from -6 to 6
- pair_v: float32 [7, 768], P(None, 'dev'), may hold values from 0.1 to 10
- fetch: int32 [32, 9], P('dev'), may hold values from 0 to 7
- pair_sides: int32 [768, 2], P('dev'), may hold values from 0 to 8, as said below
- pair_count: int32 [32], P('dev'), may hold values from 6 to 24, as said below
Outputs:
- new_depth: float32 [256, 12544], P('dev')
- new_image_params: float32 [7, 256], P(None, 'dev')
- new_pair_params: float32 [7, 768], P(None, 'dev')
Inputs may be any that keep to these rules, and one draw needn't show every extreme that they name: `pair_sides`: the two positions of a slot differ. The first slot of every holder has second position 8. `pair_count`: each holder has at least a quarter of its slots live, and some holder has all 24 live.
All inputs are finite; a program needn't handle non-finite values.
Results may differ from a plain program's by a relative error of at most 0.0003.
Values may be sent and summed in bfloat16 or wider, within the bound.
A program may use at most 128 MiB of HBM per device.

v0:
```python
import functools

import jax
import jax.numpy as jnp
from jax import lax
from jax.experimental import pallas as pl
from jax.experimental.pallas import tpu as pltpu
from jax.sharding import PartitionSpec as P

IMG_SIDE = 112
REACH = 4
ITERS = 2
WIDTH = 2 * REACH + 1
LANES = 128

focal_base = 100.0
learn_rate = 0.05
beta_one = 0.9
beta_two = 0.999
adam_epsilon = 1e-08
adam_start = 20

MESH = pl.DeviceIdType.MESH
VMEM = pl.BlockSpec(memory_space=pltpu.VMEM)
VMEM_LIMIT = 48 * 1024 * 1024


def rotation(vector):
    xval, yval, zval = vector
    scale = 1.0 / (1.0 + xval * xval + yval * yval + zval * zval)
    return [
        [
            (1.0 + xval * xval - yval * yval - zval * zval) * scale,
            2.0 * (xval * yval - zval) * scale,
            2.0 * (xval * zval + yval) * scale,
        ],
        [
            2.0 * (xval * yval + zval) * scale,
            (1.0 - xval * xval + yval * yval - zval * zval) * scale,
            2.0 * (yval * zval - xval) * scale,
        ],
        [
            2.0 * (xval * zval - yval) * scale,
            2.0 * (yval * zval + xval) * scale,
            (1.0 - xval * xval - yval * yval + zval * zval) * scale,
        ],
    ]


def coefficients(image, pair):
    spin = rotation(image[0:3])
    turn = rotation(pair[0:3])
    scale = jnp.exp(pair[6])
    out = []
    for row in range(3):
        for col in range(3):
            out.append(scale * sum(spin[m][row] * turn[m][col] for m in range(3)))
    for row in range(3):
        out.append(sum(spin[m][row] * (scale * pair[3 + m] - image[3 + m]) for m in range(3)))
    out.append(jnp.exp(-image[6]) / focal_base)
    return out


def adam_step(param, grad, moment, second, count):
    moment = beta_one * moment + (1.0 - beta_one) * grad
    second = beta_two * second + (1.0 - beta_two) * grad * grad
    fix_one = 1.0 - beta_one**count
    fix_two = 1.0 - beta_two**count
    param = param - learn_rate * (moment / fix_one) / (jnp.sqrt(second / fix_two) + adam_epsilon)
    return (param, moment, second)


def shift(n, pos):
    return (n // 2) if pos == 2 * REACH else (pos - REACH) % n


def greet(n):
    me = lax.axis_index("dev")
    steps = sorted({shift(n, pos) for pos in range(WIDTH)} | {(n - shift(n, pos)) % n for pos in range(WIDTH)})
    steps = [step for step in steps if step != 0]
    barrier = pltpu.get_barrier_semaphore()
    for step in steps:
        pl.semaphore_signal(barrier, inc=1, device_id=(lax.rem(me + step, n),), device_id_type=MESH)
    pl.semaphore_wait(barrier, len(steps))


def exchange(n, to_owner, sent, got, send_sem, recv_sem):
    me = lax.axis_index("dev")
    copies = []
    for pos in range(WIDTH):
        step = shift(n, pos)
        if step == 0:
            continue
        target = lax.rem(me + (step if to_owner else n - step), n)
        copy = pltpu.make_async_remote_copy(
            src_ref=sent.at[pos],
            dst_ref=got.at[pos],
            send_sem=send_sem.at[pos],
            recv_sem=recv_sem.at[pos],
            device_id=(target,),
            device_id_type=MESH,
        )
        copy.start()
        copies.append(copy)
    got[REACH] = sent[REACH]
    for copy in copies:
        copy.wait()


def tile_loop(tiles, body):
    step = next(s for s in (7, 4, 2, 1) if tiles % s == 0)

    def several(outer, carry):
        for inner in range(step):
            body(outer * step + inner)
        return carry

    lax.fori_loop(0, tiles // step, several, 0)


def lane_tile(index):
    return pl.ds(pl.multiple_of(index * LANES, LANES), LANES)


def send_images(n, rows, tiles, depth_ref, par_ref, served, turned, sent, got, wide_ref, par_out, sems):
    count = depth_ref.shape[0]
    pad = (tiles // 8) * 8
    for img in range(count):
        turned[img * rows + pad : (img + 1) * rows, :] = jnp.zeros((rows - pad, LANES), jnp.float32)

    def turn(index):
        turned[pl.ds(index, count, stride=rows), :] = depth_ref[:, lane_tile(index)]

    tile_loop(tiles, turn)
    turned[pl.ds(tiles, count, stride=rows), :] = par_ref[...]
    for pos in range(WIDTH):
        total = jnp.zeros((rows, LANES), jnp.float32)
        for img in range(count):
            chosen = served[pos, 0:1, :] == img
            total = jnp.where(chosen, turned[img * rows : (img + 1) * rows, :], total)
        sent[pos] = total.astype(jnp.bfloat16)
    exchange(n, False, sent, got, *sems)
    for pos in range(WIDTH):
        turned[pos * rows : (pos + 1) * rows, :] = got[pos].astype(jnp.float32)
    turned[WIDTH * rows : 16 * rows, :] = jnp.zeros(((16 - WIDTH) * rows, LANES), jnp.float32)

    def back(index):
        for half in range(2):
            wide_ref[half * 8 : half * 8 + 8, lane_tile(index)] = turned[
                pl.ds(half * 8 * rows + index, 8, stride=rows), :
            ]

    tile_loop(tiles, back)
    for half in range(2):
        par_out[half * 8 : half * 8 + 8, :] = turned[pl.ds(half * 8 * rows + tiles, 8, stride=rows), :]


def return_grads(n, rows, tiles, count, grad_ref, pgrad_ref, served, turned, sent, got, sems, update, update_params):
    pad = (tiles // 8) * 8
    for pos in range(16):
        turned[pos * rows + pad : (pos + 1) * rows, :] = jnp.zeros((rows - pad, LANES), jnp.float32)

    def turn(index):
        for half in range(2):
            turned[pl.ds(half * 8 * rows + index, 8, stride=rows), :] = grad_ref[
                half * 8 : half * 8 + 8, lane_tile(index)
            ]

    tile_loop(tiles, turn)
    for half in range(2):
        turned[pl.ds(half * 8 * rows + tiles, 8, stride=rows), :] = pgrad_ref[half * 8 : half * 8 + 8, :]
    for pos in range(WIDTH):
        sent[pos] = turned[pos * rows : (pos + 1) * rows, :].astype(jnp.bfloat16)
    exchange(n, True, sent, got, *sems)
    for pos in range(WIDTH):
        turned[pos * rows : (pos + 1) * rows, :] = got[pos].astype(jnp.float32)
    local = lax.broadcasted_iota(jnp.int32, (count, LANES), 0)
    table = [(served[pos, 0:1, :] == local).astype(jnp.float32) for pos in range(WIDTH)]

    def combine(index):
        total = table[0] * turned[pl.ds(index, 1), :]
        for pos in range(1, WIDTH):
            total = total + table[pos] * turned[pl.ds(pos * rows + index, 1), :]
        return total

    tile_loop(tiles, lambda index: update(index, combine(index)))
    update_params(combine(tiles))


def first_kernel(n, rows, tiles, wanted, depth, par, wide, par_out, served, turned, sent, got, ss, rs, fs, fr):
    greet(n)
    exchange(n, True, wanted, served, fs, fr)
    send_images(n, rows, tiles, depth, par, served, turned, sent, got, wide, par_out, (ss, rs))


def middle_kernel(
    n, rows, tiles, count, grad, pgrad, served, depth, mom, sec, par, pmom, psec,
    wide, par_out, depth_n, mom_n, sec_n, par_n, pmom_n, psec_n,
    turned, sent, got, sent_b, got_b, ss, rs, bs, br,
):
    greet(n)

    def update(index, total):
        lane = lane_tile(index)
        depth_n[:, lane], mom_n[:, lane], sec_n[:, lane] = adam_step(
            depth[:, lane], total, mom[:, lane], sec[:, lane], count
        )

    def update_params(total):
        par_n[...], pmom_n[...], psec_n[...] = adam_step(par[...], total, pmom[...], psec[...], count)

    images = depth.shape[0]
    return_grads(n, rows, tiles, images, grad, pgrad, served, turned, sent_b, got_b, (bs, br), update, update_params)
    send_images(n, rows, tiles, depth_n, par_n, served, turned, sent, got, wide, par_out, (ss, rs))


def last_kernel(
    n, rows, tiles, count, grad, pgrad, served, depth, mom, sec, par, pmom, psec,
    depth_n, par_n, turned, sent, got, ss, rs,
):
    greet(n)

    def update(index, total):
        lane = lane_tile(index)
        depth_n[:, lane] = adam_step(depth[:, lane], total, mom[:, lane], sec[:, lane], count)[0]

    def update_params(total):
        par_n[...] = adam_step(par[...], total, pmom[...], psec[...], count)[0]

    images = depth.shape[0]
    return_grads(n, rows, tiles, images, grad, pgrad, served, turned, sent, got, (ss, rs), update, update_params)


def grad_kernel(chunks, pixels, pts, conf, wide, par, pair, pick, spread, cols, rows_, grad, pgrad, tgrad,
                coef, acc, gathered, held):
    step = pl.program_id(0)
    terms = pick.shape[0]
    width = wide.shape[1]

    def columns():
        mine = jnp.dot(pick[...], par[...].astype(jnp.bfloat16), preferred_element_type=jnp.float32)
        image = [mine[:, c : c + 1] for c in range(7)]
        other = [pair[:, c : c + 1] for c in range(7)]
        return image, other

    @pl.when(step == 0)
    def _():
        image, other = columns()
        for where, value in enumerate(coefficients(image, other)):
            coef[where] = jnp.broadcast_to(value, (terms, LANES))
        acc[...] = jnp.zeros_like(acc)

    gathered[...] = jnp.dot(pick[...], wide[...].astype(jnp.bfloat16), preferred_element_type=jnp.float32)
    for group in range(terms // 8):
        part = slice(group * 8, group * 8 + 8)
        cf = [coef[where, part, :] for where in range(13)]

        def tile(index, sums):
            lane = lane_tile(index)
            dep = jnp.exp(gathered[part, lane])
            point = [pts[j, part, lane] for j in range(3)]
            weight = conf[part, lane]
            fdep = dep * cf[12]
            camera = [fdep * cols[0:1, lane], fdep * rows_[0:1, lane], dep]
            fresh = []
            forces = []
            for i in range(3):
                aim = cf[3 * i] * point[0] + cf[3 * i + 1] * point[1] + (cf[3 * i + 2] * point[2] + cf[9 + i])
                forces.append(weight * (camera[i] - aim))
            for i in range(3):
                for j in range(3):
                    fresh.append(sums[3 * i + j] + forces[i] * point[j])
            for i in range(3):
                fresh.append(sums[9 + i] + forces[i])
            bend = forces[0] * camera[0] + forces[1] * camera[1]
            fresh.append(sums[12] + bend)
            held[part, lane] = bend + forces[2] * dep
            return tuple(fresh)

        def pair_of_tiles(index, sums):
            return tile(2 * index + 1, tile(2 * index, sums))

        sums = tuple(acc[where, part, :] for where in range(13))
        sums = lax.fori_loop(0, width // (2 * LANES), pair_of_tiles, sums)
        for where in range(13):
            acc[where, part, :] = sums[where]

    factor = 2.0 / pixels
    grad[...] = jnp.dot(
        spread[...], (held[...] * factor).astype(jnp.bfloat16), preferred_element_type=jnp.float32
    )

    @pl.when(step == chunks - 1)
    def _():
        image, other = columns()
        back = jax.vjp(coefficients, image, other)[1]
        total = [jnp.sum(acc[where], axis=1, keepdims=True) * factor for where in range(13)]
        focal = jnp.exp(image[6]) * focal_base
        image_g, other_g = back([-total[where] for where in range(12)] + [total[12] * focal])
        lane = lax.broadcasted_iota(jnp.int32, (terms, LANES), 1)
        whole = jnp.zeros((terms, LANES), jnp.float32)
        pairs = jnp.zeros((terms, LANES), jnp.float32)
        for c in range(7):
            whole = jnp.where(lane == c, image_g[c], whole)
            pairs = jnp.where(lane == c, other_g[c], pairs)
        pgrad[...] = jnp.dot(
            spread[...].astype(jnp.float32), whole, preferred_element_type=jnp.float32,
            precision=lax.Precision.HIGHEST,
        )
        tgrad[...] = pairs


def term_grads(points, conf, wide, par, pair, pick, spread, cols, rows_):
    _, terms, pixels = points.shape
    tiles = pixels // LANES
    chunks = next(c for c in (7, 4, 2, 1) if tiles % c == 0)
    width = pixels // chunks
    fixed = lambda shape: pl.BlockSpec(shape, lambda c: (0,) * len(shape))
    moving = lambda lead: pl.BlockSpec((lead, width), lambda c: (0, c))
    return pl.pallas_call(
        functools.partial(grad_kernel, chunks, pixels),
        grid=(chunks,),
        in_specs=[
            pl.BlockSpec((3, terms, width), lambda c: (0, 0, c)),
            moving(terms), moving(16), fixed((16, LANES)), fixed((terms, 8)),
            fixed((terms, 16)), fixed((16, terms)), moving(8), moving(8),
        ],
        out_specs=[moving(16), fixed((16, LANES)), fixed((terms, LANES))],
        out_shape=[
            jax.ShapeDtypeStruct((16, pixels), jnp.float32),
            jax.ShapeDtypeStruct((16, LANES), jnp.float32),
            jax.ShapeDtypeStruct((terms, LANES), jnp.float32),
        ],
        scratch_shapes=[
            pltpu.VMEM((13, terms, LANES), jnp.float32),
            pltpu.VMEM((13, terms, LANES), jnp.float32),
            pltpu.VMEM((terms, width), jnp.float32),
            pltpu.VMEM((terms, width), jnp.float32),
        ],
        compiler_params=pltpu.CompilerParams(vmem_limit_bytes=VMEM_LIMIT),
    )(points, conf, wide, par, pair, pick, spread, cols, rows_)


def on_device(
    log_depth, depth_m, depth_v, image_params, image_m, image_v,
    pair_points, pair_conf, pair_params, pair_m, pair_v, fetch, pair_sides, pair_count,
):
    n = lax.axis_size("dev")
    images, pixels = log_depth.shape
    slots = pair_sides.shape[0]
    terms = 2 * slots
    tiles = pixels // LANES
    rows = -(-(tiles + 1) // 16) * 16
    f32 = jnp.float32
    as_rows = lambda a: jnp.pad(a.T, ((0, 0), (0, LANES - 7)))
    par, pmom, psec = as_rows(image_params), as_rows(image_m), as_rows(image_v)
    wanted = jnp.broadcast_to(fetch[0][:, None, None], (WIDTH, 8, LANES))

    slot_shape = jax.ShapeDtypeStruct((WIDTH, 8, LANES), jnp.int32)
    big = jax.ShapeDtypeStruct((images, pixels), f32)
    small = jax.ShapeDtypeStruct((images, LANES), f32)
    wide_shape = [jax.ShapeDtypeStruct((16, pixels), f32), jax.ShapeDtypeStruct((16, LANES), f32)]
    message = pltpu.VMEM((WIDTH, rows, LANES), jnp.bfloat16)
    sem = pltpu.SemaphoreType.DMA((WIDTH,))
    turned = pltpu.VMEM((16 * rows, LANES), f32)

    def call(kernel, ident, outs, scratch, *args):
        return pl.pallas_call(
            kernel,
            out_shape=outs,
            in_specs=[VMEM] * len(args),
            out_specs=[VMEM] * len(outs),
            scratch_shapes=scratch,
            compiler_params=pltpu.CompilerParams(
                collective_id=ident, has_side_effects=True, vmem_limit_bytes=VMEM_LIMIT
            ),
        )(*args)

    wide, wide_par, served = call(
        functools.partial(first_kernel, n, rows, tiles), 0, wide_shape + [slot_shape],
        [turned, message, message, sem, sem, sem, sem], wanted, log_depth, par,
    )

    live = (jnp.arange(slots, dtype=jnp.int32) < pair_count[0]).astype(f32)
    conf = (pair_conf.astype(f32) * live[:, None, None]).reshape(terms, pixels)
    points = pair_points.transpose(2, 0, 1, 3).astype(f32).reshape(3, terms, pixels)
    flat = pair_sides.reshape(-1)
    places = jnp.arange(16, dtype=jnp.int32)
    pick = (flat[:, None] == places[None, :]).astype(jnp.bfloat16)
    spread = (places[:, None] == flat[None, :]).astype(jnp.bfloat16)
    position = jnp.arange(pixels, dtype=jnp.int32)
    centre = (IMG_SIDE - 1) / 2.0
    cols = jnp.broadcast_to(((position % IMG_SIDE).astype(f32) - centre)[None, :], (8, pixels))
    rows_ = jnp.broadcast_to(((position // IMG_SIDE).astype(f32) - centre)[None, :], (8, pixels))

    for step_id in range(ITERS):
        pair = jnp.repeat(jnp.pad(pair_params.T, ((0, 0), (0, 1))), 2, axis=0)
        grad, pgrad, tgrad = term_grads(points, conf, wide, wide_par, pair, pick, spread, cols, rows_)
        grad_pair = tgrad[:, :7].reshape(slots, 2, 7).sum(axis=1).T
        count = adam_start + step_id + 1
        pair_params, pair_m, pair_v = adam_step(pair_params, grad_pair, pair_m, pair_v, count)
        args = (grad, pgrad, served, log_depth, depth_m, depth_v, par, pmom, psec)
        if step_id < ITERS - 1:
            wide, wide_par, log_depth, depth_m, depth_v, par, pmom, psec = call(
                functools.partial(middle_kernel, n, rows, tiles, count), 1 + step_id,
                wide_shape + [big, big, big, small, small, small],
                [turned, message, message, message, message, sem, sem, sem, sem], *args,
            )
        else:
            log_depth, par = call(
                functools.partial(last_kernel, n, rows, tiles, count), 1 + step_id, [big, small],
                [turned, message, message, sem, sem], *args,
            )
    return (log_depth, par[:, :7].T, pair_params)


def solution(mesh):
    return jax.shard_map(
        on_device,
        mesh=mesh,
        in_specs=(
            P("dev", None),
            P("dev", None),
            P("dev", None),
            P(None, "dev"),
            P(None, "dev"),
            P(None, "dev"),
            P("dev", None, None, None),
            P("dev", None, None),
            P(None, "dev"),
            P(None, "dev"),
            P(None, "dev"),
            P("dev", None),
            P("dev", None),
            P("dev"),
        ),
        out_specs=(P("dev", None), P(None, "dev"), P(None, "dev")),
        check_vma=False,
    )
```

profile of v0, /device:TPU:0, one launch (start us, length us, event | category | flops | bytes accessed | tf_op | source)
XLA Modules:
  0.0 117.3 jit_solution(5397203929077320625)
XLA Ops:
  0.6 7.4 %convert_bitcast_fusion = f32[3,24,2,12544]{3,2,0,1:T(2,128)} fusion(bf16[24,2,3,12544]{3,1,2,0:T(2,128)(2,1)} %param.20), kind=kLoop, calls=%fused_computation | loop fusion | flops 1806336 | bytes 10838016 | tf_op jit(solution)/shard_map/reshape | solution.py:386
  8.0 6.5 %copy.44 = f32[3,24,2,12544]{3,2,1,0:T(2,128)} copy(f32[3,24,2,12544]{3,2,0,1:T(2,128)} %convert_bitcast_fusion) | data formatting | bytes 14450688 | tf_op jit(solution)/shard_map/reshape | solution.py:386
  14.6 0.0 copy-start.16
  14.6 9.4 %reshape.66.pts = f32[3,48,12544]{2,1,0:T(8,128)} reshape(f32[3,24,2,12544]{3,2,1,0:T(2,128)} %copy.44) | data formatting | bytes 14450688 | tf_op jit(solution)/shard_map/reshape | solution.py:386
  24.6 0.0 copy-done.16
  24.6 2.4 %convert_multiply_fusion = f32[24,2,12544]{2,1,0:T(2,128)} fusion(bf16[24,2,12544]{2,1,0:T(2,128)(2,1)S(1)} %copy-done.16, f32[24]{0:T(128)S(1)} %compare_convert_fusion), kind=kLoop, calls=%fused_computation.1 | loop fusion | flops 1204224 | bytes 3612768 | tf_op jit(solution)/shard_map/mul | solution.py:385
  27.0 0.0 copy-start.24
  27.0 0.0 copy-start.20
  27.0 0.0 copy-start
  27.0 0.0 copy-start.17
  27.0 0.0 copy-start.23
  27.0 3.0 %reshape.60.conf = f32[48,12544]{1,0:T(8,128)S(1)} reshape(f32[24,2,12544]{2,1,0:T(2,128)} %convert_multiply_fusion) | data formatting | bytes 4816896 | tf_op jit(solution)/shard_map/reshape | solution.py:385
  30.1 0.0 copy-done.24
  30.1 0.1 broadcast_in_dim.33.wanted
  30.1 0.0 copy-done.20
  30.2 0.1 copy.45
  30.2 0.0 copy-done
  30.2 18.7 %shard_map.157 = (f32[16,12544]{1,0:T(8,128)S(1)}, f32[16,128]{1,0:T(8,128)S(1)}, s32[9,8,128]{2,1,0:T(8,128)S(1)}) custom-call(s32[9,8,128]{2,1,0:T(8,128)S(1)} %broadcast_in_dim.33.wanted, f32[8,12544]{1,0:T(8,128)S(1)} %copy-done, f32[8,128]{1,0:T(8,128)S(1)} %pad.17.par), custom_call_target="tpu_custom_call" | custom-call | tf_op jit(solution)/shard_map/pallas_call | solution.py:368
  49.0 0.0 copy-start.6
  49.0 0.9 copy-done.6
  49.9 0.0 copy-done.17
  49.9 0.1 copy.54
  50.0 0.0 copy-done.23
  50.0 0.1 copy.47
  50.1 0.1 eq.30
  50.2 0.1 fusion.9.pick
  50.4 0.0 copy-start.7
  50.4 1.1 copy-done.7
  51.6 0.0 copy-start.21
  51.6 0.0 copy-start.22
  51.6 0.0 copy-start.18
  51.6 0.0 copy-start.19
  51.6 14.6 %shard_map.158 = (f32[16,12544]{1,0:T(8,128)S(1)}, f32[16,128]{1,0:T(8,128)S(1)}, f32[48,128]{1,0:T(8,128)S(1)}) custom-call(f32[3,48,12544]{2,1,0:T(8,128)} %reshape.66.pts, f32[48,12544]{1,0:T(8,128)S(1)} %reshape.60.conf, f32[16,12544]{1,0:T(8,128)S(1)} %copy-done.7, f32[16,128]{1,0:T(8,128)S(1)} %get-tuple-element.23.par, f32[48,8]{1,0:T(8,128)S(1)} %bitcast.45, ...), custom_call_target="tpu_custom_call" | custom-call | tf_op jit(solution)/shard_map/pallas_call | solution.py:320
  66.2 0.0 copy-start.2
  66.2 0.9 copy-done.2
  67.1 0.0 copy-done.21
  67.1 0.1 copy.48
  67.2 0.0 copy-done.22
  67.2 0.1 copy.49
  67.3 1.0 copy-done.1
  68.3 1.1 copy-done.3
  69.5 1.0 copy-done.8
  70.5 1.0 copy-done.9
  71.4 15.0 %shard_map.159 = (f32[16,12544]{1,0:T(8,128)S(1)}, f32[16,128]{1,0:T(8,128)S(1)}, f32[8,12544]{1,0:T(8,128)S(1)}, f32[8,12544]{1,0:T(8,128)S(1)}, f32[8,12544]{1...) custom-call(f32[16,12544]{1,0:T(8,128)S(1)} %copy-done.3, ...), custom_call_target="tpu_custom_call" | custom-call | tf_op jit(solution)/shard_map/pallas_call | solution.py:368
  86.5 0.0 copy-start.4
  86.5 0.9 copy-done.4
  87.4 0.7 copy-done.10
  88.2 0.8 copy-done.12
  89.0 0.8 copy-done.14
  89.8 0.1 copy.50
  89.9 0.0 copy-done.18
  89.9 0.0 copy-done.19
  89.9 0.1 copy.55
  90.0 0.0 copy-start.5
  90.0 1.1 copy-done.5
  91.2 14.7 %shard_map.160 = (f32[16,12544]{1,0:T(8,128)S(1)}, f32[16,128]{1,0:T(8,128)S(1)}, f32[48,128]{1,0:T(8,128)S(1)}) custom-call(f32[3,48,12544]{2,1,0:T(8,128)} %reshape.66.pts, f32[48,12544]{1,0:T(8,128)S(1)} %reshape.60.conf, f32[16,12544]{1,0:T(8,128)S(1)} %copy-done.5, f32[16,128]{1,0:T(8,128)S(1)} %get-tuple-element.28.par, f32[48,8]{1,0:T(8,128)S(1)} %bitcast.46, ...), custom_call_target="tpu_custom_call" | custom-call | tf_op jit(solution)/shard_map/pallas_call | solution.py:320
  105.9 0.0 copy-done.11
  105.9 0.0 copy-done.13
  105.9 0.0 copy-done.15
  105.9 9.2 %shard_map.161 = (f32[8,12544]{1,0:T(8,128)S(1)}, f32[8,128]{1,0:T(8,128)S(1)}) custom-call(f32[16,12544]{1,0:T(8,128)S(1)} %get-tuple-element.30.grad, f32[16,128]{1,0:T(8,128)S(1)} %get-tuple-element.31.pgrad, s32[9,8,128]{2,1,0:T(8,128)S(1)} %get-tuple-element.26.served, f32[8,12544]{1,0:T(8,128)S(1)} %copy-done.11, f32[8,12544]{1,0:T(8,128)S(1)} %copy-done.13, ...), custom_call_target="tpu_custom_call" | custom-call | tf_op jit(solution)/shard_map/pallas_call | solution.py:368
  115.1 0.7 copy.53
  115.8 0.1 copy.52
  115.9 0.6 fusion.17
  116.5 0.7 copy.58
  (27 shorter events, 0.3 us)
Async XLA Ops:
  14.6 10.0 %copy-start.16 = (bf16[24,2,12544]{2,1,0:T(2,128)(2,1)S(1)}, bf16[24,2,12544]{2,1,0:T(2,128)(2,1)}, u32[]{:S(2)}) copy-start(bf16[24,2,12544]{2,1,0:T(2,128)(2,1)} %param.21) | copy-start | bytes 3612676
  27.0 3.0 %copy-start.24 = (s32[1,9]{1,0:T(1,128)S(1)}, s32[1,9]{1,0:T(1,128)}, u32[]{:S(2)}) copy-start(s32[1,9]{1,0:T(1,128)} %param.25) | copy-start | bytes 112
  27.0 3.1 %copy-start.20 = (f32[7,8]{1,0:T(8,128)S(1)}, f32[7,8]{1,0:T(8,128)}, u32[]{:S(2)}) copy-start(f32[7,8]{1,0:T(8,128)} %param.17) | copy-start | bytes 676
  27.0 3.2 %copy-start = (f32[8,12544]{1,0:T(8,128)S(1)}, f32[8,12544]{1,0:T(8,128)}, u32[]{:S(2)}) copy-start(f32[8,12544]{1,0:T(8,128)} %depth.3) | copy-start | bytes 1204228
  27.0 22.9 %copy-start.17 = (f32[7,24]{1,0:T(8,128)S(1)}, f32[7,24]{1,0:T(8,128)}, u32[]{:S(2)}) copy-start(f32[7,24]{1,0:T(8,128)} %param.22) | copy-start | bytes 2020
  27.0 23.0 %copy-start.23 = (s32[24,2]{0,1:T(2,128)S(1)}, s32[24,2]{0,1:T(2,128)}, u32[]{:S(2)}) copy-start(s32[24,2]{0,1:T(2,128)} %param.26) | copy-start | bytes 580
  49.0 0.9 copy-start.6
  50.4 1.1 copy-start.7
  51.6 15.6 %copy-start.21 = (f32[7,8]{1,0:T(8,128)S(1)}, f32[7,8]{1,0:T(8,128)}, u32[]{:S(2)}) copy-start(f32[7,8]{1,0:T(8,128)} %param.18) | copy-start | bytes 676
  51.6 15.6 %copy-start.22 = (f32[7,8]{1,0:T(8,128)S(1)}, f32[7,8]{1,0:T(8,128)}, u32[]{:S(2)}) copy-start(f32[7,8]{1,0:T(8,128)} %param.19) | copy-start | bytes 676
  51.6 38.3 %copy-start.18 = (f32[7,24]{1,0:T(8,128)S(1)}, f32[7,24]{1,0:T(8,128)}, u32[]{:S(2)}) copy-start(f32[7,24]{1,0:T(8,128)} %param.24) | copy-start | bytes 2020
  51.6 38.3 %copy-start.19 = (f32[7,24]{1,0:T(8,128)S(1)}, f32[7,24]{1,0:T(8,128)}, u32[]{:S(2)}) copy-start(f32[7,24]{1,0:T(8,128)} %param.23) | copy-start | bytes 2020
  66.2 0.9 copy-start.2
  67.3 1.0 copy-start.1
  68.3 1.1 copy-start.3
  69.4 1.0 copy-start.8
  70.4 1.0 copy-start.9
  86.5 0.9 copy-start.4
  87.4 0.7 copy-start.10
  88.2 0.8 copy-start.12
  89.0 0.8 copy-start.14
  90.0 1.1 copy-start.5
  91.2 14.7 %copy-start.11 = (f32[8,12544]{1,0:T(8,128)S(1)}, f32[8,12544]{1,0:T(8,128)}, u32[]{:S(2)}) copy-start(f32[8,12544]{1,0:T(8,128)} %copy-done.10) | copy-start | bytes 1204228
  91.2 14.7 %copy-start.13 = (f32[8,12544]{1,0:T(8,128)S(1)}, f32[8,12544]{1,0:T(8,128)}, u32[]{:S(2)}) copy-start(f32[8,12544]{1,0:T(8,128)} %copy-done.12) | copy-start | bytes 1204228
  91.2 14.7 %copy-start.15 = (f32[8,12544]{1,0:T(8,128)S(1)}, f32[8,12544]{1,0:T(8,128)}, u32[]{:S(2)}) copy-start(f32[8,12544]{1,0:T(8,128)} %copy-done.14) | copy-start | bytes 1204228
where the time goes:
time: 118 us; the launch traced here: 117 us
  Pallas kernels  72.3 us (61%)
  local copies, waits for them, and re-layouts  32.8 us (28%)
  other arithmetic  10.7 us (9%)
  between operations  1.53 us (1%)
    pallas_call x3, Pallas kernels, call(): pl.pallas_call(kernel, out_shape=outs, in_specs=[VMEM] * len(args), out_s...  43 us
    pallas_call x2, Pallas kernels, term_grads(): pl.pallas_call(functools.partial(grad_kernel, chunks, pixels), grid=(chun...  29.3 us
    reshape x2, local copies, waits for them, and re-layouts, on_device(): pair_points.transpose(2, 0, 1, 3).astype(f32).reshape(3, terms, pixels)  15.9 us
    unnamed x58, local copies, waits for them, and re-layouts  13.4 us
    reshape x1, other arithmetic, on_device(): pair_points.transpose(2, 0, 1, 3).astype(f32).reshape(3, terms, pixels)  7.41 us
    reshape x1, local copies, waits for them, and re-layouts, on_device(): conf = (pair_conf.astype(f32) * live[:, None, None]).reshape(terms, pixels)  3.01 us
    mul x1, other arithmetic, on_device(): conf = (pair_conf.astype(f32) * live[:, None, None]).reshape(terms, pixels)  2.4 us

commit v1 on v0

--- a/solution.py
+++ b/solution.py
@@ -22,7 +22,7 @@
 
 MESH = pl.DeviceIdType.MESH
 VMEM = pl.BlockSpec(memory_space=pltpu.VMEM)
-VMEM_LIMIT = 48 * 1024 * 1024
+VMEM_LIMIT = 16 * 1024 * 1024
 
 
 def rotation(vector):
@@ -74,37 +74,42 @@
     return (n // 2) if pos == 2 * REACH else (pos - REACH) % n
 
 
+def partners(n):
+    steps = {shift(n, pos) for pos in range(WIDTH)} | {(n - shift(n, pos)) % n for pos in range(WIDTH)}
+    return sorted(steps - {0})
+
+
 def greet(n):
     me = lax.axis_index("dev")
-    steps = sorted({shift(n, pos) for pos in range(WIDTH)} | {(n - shift(n, pos)) % n for pos in range(WIDTH)})
-    steps = [step for step in steps if step != 0]
     barrier = pltpu.get_barrier_semaphore()
-    for step in steps:
+    for step in partners(n):
         pl.semaphore_signal(barrier, inc=1, device_id=(lax.rem(me + step, n),), device_id_type=MESH)
-    pl.semaphore_wait(barrier, len(steps))
-
-
-def exchange(n, to_owner, sent, got, send_sem, recv_sem):
+
+
+def await_partners(n):
+    pl.semaphore_wait(pltpu.get_barrier_semaphore(), len(partners(n)))
+
+
+ORDER = [2 * REACH] + sorted(range(2 * REACH), key=lambda pos: -abs(pos - REACH))
+
+
+def send(n, to_owner, pos, sent, got, sems):
     me = lax.axis_index("dev")
-    copies = []
-    for pos in range(WIDTH):
-        step = shift(n, pos)
-        if step == 0:
-            continue
-        target = lax.rem(me + (step if to_owner else n - step), n)
-        copy = pltpu.make_async_remote_copy(
-            src_ref=sent.at[pos],
-            dst_ref=got.at[pos],
-            send_sem=send_sem.at[pos],
-            recv_sem=recv_sem.at[pos],
-            device_id=(target,),
-            device_id_type=MESH,
-        )
-        copy.start()
-        copies.append(copy)
-    got[REACH] = sent[REACH]
-    for copy in copies:
-        copy.wait()
+    step = shift(n, pos)
+    if step == 0:
+        got[pos] = sent[pos]
+        return None
+    target = lax.rem(me + (step if to_owner else n - step), n)
+    copy = pltpu.make_async_remote_copy(
+        src_ref=sent.at[pos],
+        dst_ref=got.at[pos],
+        send_sem=sems[0].at[pos],
+        recv_sem=sems[1].at[pos],
+        device_id=(target,),
+        device_id_type=MESH,
+    )
+    copy.start()
+    return copy
 
 
 def tile_loop(tiles, body):
@@ -122,7 +127,7 @@
     return pl.ds(pl.multiple_of(index * LANES, LANES), LANES)
 
 
-def send_images(n, rows, tiles, depth_ref, par_ref, served, turned, sent, got, wide_ref, par_out, sems):
+def turn_images(rows, tiles, depth_ref, par_ref, turned):
     count = depth_ref.shape[0]
     pad = (tiles // 8) * 8
     for img in range(count):
@@ -133,14 +138,20 @@
 
     tile_loop(tiles, turn)
     turned[pl.ds(tiles, count, stride=rows), :] = par_ref[...]
-    for pos in range(WIDTH):
-        total = jnp.zeros((rows, LANES), jnp.float32)
-        for img in range(count):
+
+
+def send_images(n, rows, tiles, count, served, turned, sent, got, wide_ref, par_out, sems):
+    copies = []
+    for pos in ORDER:
+        total = turned[0:rows, :]
+        for img in range(1, count):
             chosen = served[pos, 0:1, :] == img
             total = jnp.where(chosen, turned[img * rows : (img + 1) * rows, :], total)
         sent[pos] = total.astype(jnp.bfloat16)
-    exchange(n, False, sent, got, *sems)
-    for pos in range(WIDTH):
+        copies.append((pos, send(n, False, pos, sent, got, sems)))
+    for pos, copy in copies[::-1]:
+        if copy is not None:
+            copy.wait()
         turned[pos * rows : (pos + 1) * rows, :] = got[pos].astype(jnp.float32)
     turned[WIDTH * rows : 16 * rows, :] = jnp.zeros(((16 - WIDTH) * rows, LANES), jnp.float32)
 
@@ -156,6 +167,7 @@
 
 
 def return_grads(n, rows, tiles, count, grad_ref, pgrad_ref, served, turned, sent, got, sems, update, update_params):
+    greet(n)
     pad = (tiles // 8) * 8
     for pos in range(16):
         turned[pos * rows + pad : (pos + 1) * rows, :] = jnp.zeros((rows - pad, LANES), jnp.float32)
@@ -169,10 +181,14 @@
     tile_loop(tiles, turn)
     for half in range(2):
         turned[pl.ds(half * 8 * rows + tiles, 8, stride=rows), :] = pgrad_ref[half * 8 : half * 8 + 8, :]
-    for pos in range(WIDTH):
+    await_partners(n)
+    copies = []
+    for pos in ORDER:
         sent[pos] = turned[pos * rows : (pos + 1) * rows, :].astype(jnp.bfloat16)
-    exchange(n, True, sent, got, *sems)
-    for pos in range(WIDTH):
+        copies.append((pos, send(n, True, pos, sent, got, sems)))
+    for pos, copy in copies[::-1]:
+        if copy is not None:
+            copy.wait()
         turned[pos * rows : (pos + 1) * rows, :] = got[pos].astype(jnp.float32)
     local = lax.broadcasted_iota(jnp.int32, (count, LANES), 0)
     table = [(served[pos, 0:1, :] == local).astype(jnp.float32) for pos in range(WIDTH)]
@@ -189,8 +205,13 @@
 
 def first_kernel(n, rows, tiles, wanted, depth, par, wide, par_out, served, turned, sent, got, ss, rs, fs, fr):
     greet(n)
-    exchange(n, True, wanted, served, fs, fr)
-    send_images(n, rows, tiles, depth, par, served, turned, sent, got, wide, par_out, (ss, rs))
+    await_partners(n)
+    copies = [send(n, True, pos, wanted, served, (fs, fr)) for pos in ORDER]
+    turn_images(rows, tiles, depth, par, turned)
+    for copy in copies:
+        if copy is not None:
+            copy.wait()
+    send_images(n, rows, tiles, depth.shape[0], served, turned, sent, got, wide, par_out, (ss, rs))
 
 
 def middle_kernel(
@@ -198,7 +219,6 @@
     wide, par_out, depth_n, mom_n, sec_n, par_n, pmom_n, psec_n,
     turned, sent, got, sent_b, got_b, ss, rs, bs, br,
 ):
-    greet(n)
 
     def update(index, total):
         lane = lane_tile(index)
@@ -211,14 +231,14 @@
 
     images = depth.shape[0]
     return_grads(n, rows, tiles, images, grad, pgrad, served, turned, sent_b, got_b, (bs, br), update, update_params)
-    send_images(n, rows, tiles, depth_n, par_n, served, turned, sent, got, wide, par_out, (ss, rs))
+    turn_images(rows, tiles, depth_n, par_n, turned)
+    send_images(n, rows, tiles, images, served, turned, sent, got, wide, par_out, (ss, rs))
 
 
 def last_kernel(
     n, rows, tiles, count, grad, pgrad, served, depth, mom, sec, par, pmom, psec,
     depth_n, par_n, turned, sent, got, ss, rs,
 ):
-    greet(n)
 
     def update(index, total):
         lane = lane_tile(index)
@@ -250,18 +270,20 @@
             coef[where] = jnp.broadcast_to(value, (terms, LANES))
         acc[...] = jnp.zeros_like(acc)
 
-    gathered[...] = jnp.dot(pick[...], wide[...].astype(jnp.bfloat16), preferred_element_type=jnp.float32)
+    gathered[...] = jnp.exp(
+        jnp.dot(pick[...], wide[...].astype(jnp.bfloat16), preferred_element_type=jnp.float32)
+    )
     for group in range(terms // 8):
         part = slice(group * 8, group * 8 + 8)
         cf = [coef[where, part, :] for where in range(13)]
 
         def tile(index, sums):
-            lane = lane_tile(index)
-            dep = jnp.exp(gathered[part, lane])
+            lane = slice(index * LANES, (index + 1) * LANES)
+            dep = gathered[part, lane]
             point = [pts[j, part, lane] for j in range(3)]
             weight = conf[part, lane]
             fdep = dep * cf[12]
-            camera = [fdep * cols[0:1, lane], fdep * rows_[0:1, lane], dep]
+            camera = [fdep * cols[:, lane], fdep * rows_[:, lane], dep]
             fresh = []
             forces = []
             for i in range(3):
@@ -277,11 +299,9 @@
             held[part, lane] = bend + forces[2] * dep
             return tuple(fresh)
 
-        def pair_of_tiles(index, sums):
-            return tile(2 * index + 1, tile(2 * index, sums))
-
         sums = tuple(acc[where, part, :] for where in range(13))
-        sums = lax.fori_loop(0, width // (2 * LANES), pair_of_tiles, sums)
+        for index in range(width // LANES):
+            sums = tile(index, sums)
         for where in range(13):
             acc[where, part, :] = sums[where]
 
@@ -310,6 +330,40 @@
         tgrad[...] = pairs
 
 
+def spread_kernel(raw_points, raw_conf, live, points, conf):
+    for slot in range(raw_points.shape[0]):
+        part = slice(2 * slot, 2 * slot + 2)
+        for j in range(3):
+            points[j, part, :] = raw_points[slot, j].astype(jnp.float32)
+        conf[part, :] = raw_conf[slot].astype(jnp.float32) * live[part, 0:1]
+
+
+def spread_pairs(pair_points, pair_conf, live):
+    slots, _, _, pixels = pair_points.shape
+    terms = 2 * slots
+    tiles = pixels // LANES
+    chunks = next(c for c in (7, 4, 2, 1) if tiles % c == 0)
+    width = pixels // chunks
+    return pl.pallas_call(
+        spread_kernel,
+        grid=(chunks,),
+        in_specs=[
+            pl.BlockSpec((slots, 3, 2, width), lambda c: (0, 0, 0, c)),
+            pl.BlockSpec((slots, 2, width), lambda c: (0, 0, c)),
+            pl.BlockSpec((terms, LANES), lambda c: (0, 0)),
+        ],
+        out_specs=[
+            pl.BlockSpec((3, terms, width), lambda c: (0, 0, c)),
+            pl.BlockSpec((terms, width), lambda c: (0, c)),
+        ],
+        out_shape=[
+            jax.ShapeDtypeStruct((3, terms, pixels), jnp.float32),
+            jax.ShapeDtypeStruct((terms, pixels), jnp.float32),
+        ],
+        compiler_params=pltpu.CompilerParams(vmem_limit_bytes=VMEM_LIMIT),
+    )(pair_points.transpose(0, 2, 1, 3), pair_conf, live)
+
+
 def term_grads(points, conf, wide, par, pair, pick, spread, cols, rows_):
     _, terms, pixels = points.shape
     tiles = pixels // LANES
@@ -382,8 +436,8 @@
     )
 
     live = (jnp.arange(slots, dtype=jnp.int32) < pair_count[0]).astype(f32)
-    conf = (pair_conf.astype(f32) * live[:, None, None]).reshape(terms, pixels)
-    points = pair_points.transpose(2, 0, 1, 3).astype(f32).reshape(3, terms, pixels)
+    live = jnp.broadcast_to(jnp.repeat(live, 2)[:, None], (terms, LANES))
+    points, conf = spread_pairs(pair_points, pair_conf, live)
     flat = pair_sides.reshape(-1)
     places = jnp.arange(16, dtype=jnp.int32)
     pick = (flat[:, None] == places[None, :]).astype(jnp.bfloat16)

time: 118 us -> 91.3 us (0.77)
  local copies, waits for them, and re-layouts: 32.8 us -> 19 us
  other arithmetic: 10.7 us -> 0.85 us
  Pallas kernels: 72.3 us -> 69.4 us
    reshape x3 -> x0, local copies, waits for them, and re-layouts: 18.9 us -> none  [the longest x2 15.9 us: on_device(): pair_points.transpose(2, 0, 1, 3).astype(f32).reshape(3, terms, pixels)]
    pallas_call x2, Pallas kernels: 29.3 us -> 21.7 us  [term_grads(): pl.pallas_call(functools.partial(grad_kernel, chunks, pixels), grid=(chun...]
    reshape x1 -> x0, other arithmetic: 7.41 us -> none  [on_device(): pair_points.transpose(2, 0, 1, 3).astype(f32).reshape(3, terms, pixels)]
    unnamed x58 -> x34, local copies, waits for them, and re-layouts: 13.4 us -> 17.7 us
    pallas_call x0 -> x1, Pallas kernels: none -> 3.97 us  [spread_pairs(): pl.pallas_call(spread_kernel, grid=(chunks,), in_specs=[pl.BlockSpec((slo...]
    mul x1 -> x0, other arithmetic: 2.4 us -> none  [on_device(): conf = (pair_conf.astype(f32) * live[:, None, None]).reshape(terms, pixels)]
where the time goes in v1:
time: 91.3 us; the launch traced here: 90.7 us
  Pallas kernels  69.4 us (76%)
  local copies, waits for them, and re-layouts  19 us (21%)
  between operations  1.5 us (2%)
    pallas_call x3, Pallas kernels, call(): pl.pallas_call(kernel, out_shape=outs, in_specs=[VMEM] * len(args), out_s...  43.7 us
    pallas_call x2, Pallas kernels, term_grads(): pl.pallas_call(functools.partial(grad_kernel, chunks, pixels), grid=(chun...  21.7 us
    unnamed x34, local copies, waits for them, and re-layouts  17.7 us
    pallas_call x1, Pallas kernels, spread_pairs(): pl.pallas_call(spread_kernel, grid=(chunks,), in_specs=[pl.BlockSpec((slo...  3.97 us

profile of v1, /device:TPU:0, one launch (start us, length us, event | category | flops | bytes accessed | tf_op | source)
XLA Modules:
  0.0 90.7 jit_solution(1106956428905829446)
XLA Ops:
  1.3 0.8 copy.41
  2.1 0.8 copy.44
  2.8 0.8 copy.45
  3.6 0.1 broadcast_in_dim.41
  3.7 0.1 broadcast_in_dim.42
  3.8 0.8 copy.43
  4.5 0.1 eq.30
  4.6 0.1 fusion.9.pick
  4.7 0.8 copy.50
  5.5 0.1 broadcast_in_dim.43.live
  5.6 0.7 broadcast_in_dim.45.wanted
  6.4 0.0 copy-start.3
  6.5 1.0 %copy-done.3 = f32[8,12544]{1,0:T(8,128)S(1)} copy-done((f32[8,12544]{1,0:T(8,128)S(1)}, f32[8,12544]{1,0:T(8,128)}, u32[]{:S(2)}) %copy-start.3) | copy-done | bytes 401432
  7.4 18.7 %shard_map.158 = (f32[16,12544]{1,0:T(8,128)S(1)}, f32[16,128]{1,0:T(8,128)S(1)}, s32[9,8,128]{2,1,0:T(8,128)S(1)}) custom-call(s32[9,8,128]{2,1,0:T(8,128)S(1)} %broadcast_in_dim.45.wanted, f32[8,12544]{1,0:T(8,128)S(1)} %copy-done.3, f32[8,128]{1,0:T(8,128)S(1)} %pad.17.par), custom_call_target="tpu_custom_call" | custom-call | tf_op jit(solution)/shard_map/pallas_call | solution.py:422
  26.2 0.0 copy-start.2
  26.2 2.0 %copy-done.2 = bf16[24,2,3,12544]{3,1,2,0:T(2,128)(2,1)S(1)} copy-done((bf16[24,2,3,12544]{3,1,2,0:T(2,128)(2,1)S(1)}, bf16[24,2,3,12544]{3,1,2,0:T(2,128)(2,1)}, u32[]{:S(2)}) %copy-start.2) | copy-done | bytes 3612696
  28.2 0.0 copy-start.5
  28.2 1.3 %copy-done.5 = bf16[24,2,12544]{2,1,0:T(2,128)(2,1)S(1)} copy-done((bf16[24,2,12544]{2,1,0:T(2,128)(2,1)S(1)}, bf16[24,2,12544]{2,1,0:T(2,128)(2,1)}, u32[]{:S(2)}) %copy-start.5) | copy-done | bytes 1204248
  29.5 4.0 %shard_map.157 = (f32[3,48,12544]{2,1,0:T(8,128)S(1)}, f32[48,12544]{1,0:T(8,128)S(1)}) custom-call(bf16[24,3,2,12544]{3,2,1,0:T(2,128)(2,1)S(1)} %bitcast.44, bf16[24,2,12544]{2,1,0:T(2,128)(2,1)S(1)} %copy-done.5, f32[48,128]{1,0:T(8,128)S(1)} %broadcast_in_dim.43.live), custom_call_target="tpu_custom_call" | custom-call | tf_op jit(solution)/shard_map/pallas_call | solution.py:347
  33.5 0.0 copy-start
  33.5 0.0 copy-start.10
  33.5 0.0 copy-start.11
  33.5 0.0 copy-start.12
  33.5 10.9 %shard_map.159 = (f32[16,12544]{1,0:T(8,128)S(1)}, f32[16,128]{1,0:T(8,128)S(1)}, f32[48,128]{1,0:T(8,128)S(1)}) custom-call(f32[3,48,12544]{2,1,0:T(8,128)S(1)} %get-tuple-element.24.pts, f32[48,12544]{1,0:T(8,128)S(1)} %get-tuple-element.25.conf, f32[16,12544]{1,0:T(8,128)S(1)} %get-tuple-element.26.wide, f32[16,128]{1,0:T(8,128)S(1)} %get-tuple-element.27.par, ...), custom_call_target="tpu_custom_call" | custom-call | tf_op jit(solution)/shard_map/pallas_call | solution.py:374
  44.4 0.0 copy-done
  44.4 0.0 copy-start.6
  44.4 0.9 copy-done.6
  45.3 0.1 copy.46
  45.4 0.0 copy-done.10
  45.4 0.0 copy-done.11
  45.4 0.0 copy-done.12
  45.4 0.1 copy.51
  45.5 0.0 copy-start.4
  45.6 1.0 %copy-done.4 = f32[8,12544]{1,0:T(8,128)S(1)} copy-done((f32[8,12544]{1,0:T(8,128)S(1)}, f32[8,12544]{1,0:T(8,128)}, u32[]{:S(2)}) %copy-start.4) | copy-done | bytes 401432
  46.5 0.0 copy-start.7
  46.5 1.1 %copy-done.7 = f32[16,12544]{1,0:T(8,128)S(1)} copy-done((f32[16,12544]{1,0:T(8,128)S(1)}, f32[16,12544]{1,0:T(8,128)}, u32[]{:S(2)}) %copy-start.7) | copy-done | bytes 802840
  47.7 0.0 copy-start.8
  47.7 1.0 %copy-done.8 = f32[8,12544]{1,0:T(8,128)S(1)} copy-done((f32[8,12544]{1,0:T(8,128)S(1)}, f32[8,12544]{1,0:T(8,128)}, u32[]{:S(2)}) %copy-start.8) | copy-done | bytes 401432
  48.7 0.0 copy-start.9
  48.7 1.0 %copy-done.9 = f32[8,12544]{1,0:T(8,128)S(1)} copy-done((f32[8,12544]{1,0:T(8,128)S(1)}, f32[8,12544]{1,0:T(8,128)}, u32[]{:S(2)}) %copy-start.9) | copy-done | bytes 401432
  49.7 15.1 %shard_map.160 = (f32[16,12544]{1,0:T(8,128)S(1)}, f32[16,128]{1,0:T(8,128)S(1)}, f32[8,12544]{1,0:T(8,128)S(1)}, f32[8,12544]{1,0:T(8,128)S(1)}, f32[8,12544]{1...) custom-call(f32[16,12544]{1,0:T(8,128)S(1)} %copy-done.7, ...), custom_call_target="tpu_custom_call" | custom-call | tf_op jit(solution)/shard_map/pallas_call | solution.py:422
  64.8 0.0 copy-start.1
  64.8 3.0 %copy-done.1 = f32[3,48,12544]{2,1,0:T(8,128)S(1)} copy-done((f32[3,48,12544]{2,1,0:T(8,128)S(1)}, f32[3,48,12544]{2,1,0:T(8,128)}, u32[]{:S(2)}) %copy-start.1) | copy-done | bytes 7225368
  67.8 10.8 %shard_map.161 = (f32[16,12544]{1,0:T(8,128)S(1)}, f32[16,128]{1,0:T(8,128)S(1)}, f32[48,128]{1,0:T(8,128)S(1)}) custom-call(f32[3,48,12544]{2,1,0:T(8,128)S(1)} %copy-done.1, f32[48,12544]{1,0:T(8,128)S(1)} %get-tuple-element.25.conf, f32[16,12544]{1,0:T(8,128)S(1)} %get-tuple-element.31.wide, f32[16,128]{1,0:T(8,128)S(1)} %get-tuple-element.32.par, ...), custom_call_target="tpu_custom_call" | custom-call | tf_op jit(solution)/shard_map/pallas_call | solution.py:374
  78.7 9.9 %shard_map.162 = (f32[8,12544]{1,0:T(8,128)S(1)}, f32[8,128]{1,0:T(8,128)S(1)}) custom-call(f32[16,12544]{1,0:T(8,128)S(1)} %get-tuple-element.34.grad, f32[16,128]{1,0:T(8,128)S(1)} %get-tuple-element.35.pgrad, s32[9,8,128]{2,1,0:T(8,128)S(1)} %get-tuple-element.30.served, f32[8,12544]{1,0:T(8,128)S(1)} %get-tuple-element.36.depth, ...), custom_call_target="tpu_custom_call" | custom-call | tf_op jit(solution)/shard_map/pallas_call | solution.py:422
  88.6 0.7 copy.49
  89.3 0.1 copy.48
  89.4 0.6 fusion.17
  90.0 0.7 copy.54
  (17 shorter events, 0.3 us)
Async XLA Ops:
  6.4 1.0 %copy-start.3 = (f32[8,12544]{1,0:T(8,128)S(1)}, f32[8,12544]{1,0:T(8,128)}, u32[]{:S(2)}) copy-start(f32[8,12544]{1,0:T(8,128)} %depth.3) | copy-start | bytes 1204228
  26.2 2.0 %copy-start.2 = (bf16[24,2,3,12544]{3,1,2,0:T(2,128)(2,1)S(1)}, bf16[24,2,3,12544]{3,1,2,0:T(2,128)(2,1)}, u32[]{:S(2)}) copy-start(bf16[24,2,3,12544]{3,1,2,0:T(2,128)(2,1)} %param.20) | copy-start | bytes 10838020
  28.2 1.3 %copy-start.5 = (bf16[24,2,12544]{2,1,0:T(2,128)(2,1)S(1)}, bf16[24,2,12544]{2,1,0:T(2,128)(2,1)}, u32[]{:S(2)}) copy-start(bf16[24,2,12544]{2,1,0:T(2,128)(2,1)} %raw_conf.1) | copy-start | bytes 3612676
  33.5 10.9 %copy-start = (f32[3,48,12544]{2,1,0:T(8,128)}, f32[3,48,12544]{2,1,0:T(8,128)S(1)}, u32[]{:S(2)}) copy-start(f32[3,48,12544]{2,1,0:T(8,128)S(1)} %get-tuple-element.24.pts) | copy-start | bytes 21676036
  33.5 11.9 %copy-start.10 = (f32[7,24]{1,0:T(8,128)S(1)}, f32[7,24]{1,0:T(8,128)}, u32[]{:S(2)}) copy-start(f32[7,24]{1,0:T(8,128)} %param.22) | copy-start | bytes 2020
  33.5 11.9 %copy-start.11 = (f32[7,24]{1,0:T(8,128)S(1)}, f32[7,24]{1,0:T(8,128)}, u32[]{:S(2)}) copy-start(f32[7,24]{1,0:T(8,128)} %param.24) | copy-start | bytes 2020
  33.5 11.9 %copy-start.12 = (f32[7,24]{1,0:T(8,128)S(1)}, f32[7,24]{1,0:T(8,128)}, u32[]{:S(2)}) copy-start(f32[7,24]{1,0:T(8,128)} %param.23) | copy-start | bytes 2020
  44.4 0.9 copy-start.6
  45.5 1.0 %copy-start.4 = (f32[8,12544]{1,0:T(8,128)S(1)}, f32[8,12544]{1,0:T(8,128)}, u32[]{:S(2)}) copy-start(f32[8,12544]{1,0:T(8,128)} %depth.3) | copy-start | bytes 1204228
  46.5 1.1 %copy-start.7 = (f32[16,12544]{1,0:T(8,128)S(1)}, f32[16,12544]{1,0:T(8,128)}, u32[]{:S(2)}) copy-start(f32[16,12544]{1,0:T(8,128)} %copy-done.6) | copy-start | bytes 2408452
  47.7 1.0 %copy-start.8 = (f32[8,12544]{1,0:T(8,128)S(1)}, f32[8,12544]{1,0:T(8,128)}, u32[]{:S(2)}) copy-start(f32[8,12544]{1,0:T(8,128)} %mom.1) | copy-start | bytes 1204228
  48.7 1.0 %copy-start.9 = (f32[8,12544]{1,0:T(8,128)S(1)}, f32[8,12544]{1,0:T(8,128)}, u32[]{:S(2)}) copy-start(f32[8,12544]{1,0:T(8,128)} %sec.1) | copy-start | bytes 1204228
  64.8 3.1 %copy-start.1 = (f32[3,48,12544]{2,1,0:T(8,128)S(1)}, f32[3,48,12544]{2,1,0:T(8,128)}, u32[]{:S(2)}) copy-start(f32[3,48,12544]{2,1,0:T(8,128)} %copy-done) | copy-start | bytes 21676036

commit v2 on v1

--- a/solution.py
+++ b/solution.py
@@ -23,6 +23,7 @@
 MESH = pl.DeviceIdType.MESH
 VMEM = pl.BlockSpec(memory_space=pltpu.VMEM)
 VMEM_LIMIT = 16 * 1024 * 1024
+GRAD_VMEM_LIMIT = 48 * 1024 * 1024
 
 
 def rotation(vector):
@@ -112,6 +113,13 @@
     return copy
 
 
+def bring(sources, targets, sem):
+    copies = [pltpu.make_async_copy(a, b, sem.at[i]) for i, (a, b) in enumerate(zip(sources, targets))]
+    for copy in copies:
+        copy.start()
+    return copies
+
+
 def tile_loop(tiles, body):
     step = next(s for s in (7, 4, 2, 1) if tiles % s == 0)
 
@@ -166,7 +174,7 @@
         par_out[half * 8 : half * 8 + 8, :] = turned[pl.ds(half * 8 * rows + tiles, 8, stride=rows), :]
 
 
-def return_grads(n, rows, tiles, count, grad_ref, pgrad_ref, served, turned, sent, got, sems, update, update_params):
+def return_grads(n, rows, tiles, count, grad_ref, pgrad_ref, served, turned, sent, got, sems, update, update_params, loads):
     greet(n)
     pad = (tiles // 8) * 8
     for pos in range(16):
@@ -178,6 +186,7 @@
                 half * 8 : half * 8 + 8, lane_tile(index)
             ]
 
+    loads[0].wait()
     tile_loop(tiles, turn)
     for half in range(2):
         turned[pl.ds(half * 8 * rows + tiles, 8, stride=rows), :] = pgrad_ref[half * 8 : half * 8 + 8, :]
@@ -199,14 +208,20 @@
             total = total + table[pos] * turned[pl.ds(pos * rows + index, 1), :]
         return total
 
+    for load in loads[1:]:
+        load.wait()
     tile_loop(tiles, lambda index: update(index, combine(index)))
     update_params(combine(tiles))
 
 
-def first_kernel(n, rows, tiles, wanted, depth, par, wide, par_out, served, turned, sent, got, ss, rs, fs, fr):
+def first_kernel(
+    n, rows, tiles, wanted, par, depth_hbm, wide, par_out, served, turned, sent, got, ss, rs, fs, fr, depth, ls
+):
+    loads = bring([depth_hbm], [depth], ls)
     greet(n)
     await_partners(n)
     copies = [send(n, True, pos, wanted, served, (fs, fr)) for pos in ORDER]
+    loads[0].wait()
     turn_images(rows, tiles, depth, par, turned)
     for copy in copies:
         if copy is not None:
@@ -215,10 +230,11 @@
 
 
 def middle_kernel(
-    n, rows, tiles, count, grad, pgrad, served, depth, mom, sec, par, pmom, psec,
+    n, rows, tiles, count, pgrad, served, par, pmom, psec, grad_hbm, depth_hbm, mom_hbm, sec_hbm,
     wide, par_out, depth_n, mom_n, sec_n, par_n, pmom_n, psec_n,
-    turned, sent, got, sent_b, got_b, ss, rs, bs, br,
+    turned, sent, got, sent_b, got_b, ss, rs, bs, br, grad, depth, mom, sec, ls,
 ):
+    loads = bring([grad_hbm, depth_hbm, mom_hbm, sec_hbm], [grad, depth, mom, sec], ls)
 
     def update(index, total):
         lane = lane_tile(index)
@@ -230,15 +246,16 @@
         par_n[...], pmom_n[...], psec_n[...] = adam_step(par[...], total, pmom[...], psec[...], count)
 
     images = depth.shape[0]
-    return_grads(n, rows, tiles, images, grad, pgrad, served, turned, sent_b, got_b, (bs, br), update, update_params)
+    return_grads(n, rows, tiles, images, grad, pgrad, served, turned, sent_b, got_b, (bs, br), update, update_params, loads)
     turn_images(rows, tiles, depth_n, par_n, turned)
     send_images(n, rows, tiles, images, served, turned, sent, got, wide, par_out, (ss, rs))
 
 
 def last_kernel(
-    n, rows, tiles, count, grad, pgrad, served, depth, mom, sec, par, pmom, psec,
-    depth_n, par_n, turned, sent, got, ss, rs,
+    n, rows, tiles, count, pgrad, served, par, pmom, psec, grad_hbm, depth_hbm, mom_hbm, sec_hbm,
+    depth_n, par_n, turned, sent, got, ss, rs, grad, depth, mom, sec, ls,
 ):
+    loads = bring([grad_hbm, depth_hbm, mom_hbm, sec_hbm], [grad, depth, mom, sec], ls)
 
     def update(index, total):
         lane = lane_tile(index)
@@ -248,7 +265,7 @@
         par_n[...] = adam_step(par[...], total, pmom[...], psec[...], count)[0]
 
     images = depth.shape[0]
-    return_grads(n, rows, tiles, images, grad, pgrad, served, turned, sent, got, (ss, rs), update, update_params)
+    return_grads(n, rows, tiles, images, grad, pgrad, served, turned, sent, got, (ss, rs), update, update_params, loads)
 
 
 def grad_kernel(chunks, pixels, pts, conf, wide, par, pair, pick, spread, cols, rows_, grad, pgrad, tgrad,
@@ -360,7 +377,7 @@
             jax.ShapeDtypeStruct((3, terms, pixels), jnp.float32),
             jax.ShapeDtypeStruct((terms, pixels), jnp.float32),
         ],
-        compiler_params=pltpu.CompilerParams(vmem_limit_bytes=VMEM_LIMIT),
+        compiler_params=pltpu.CompilerParams(vmem_limit_bytes=GRAD_VMEM_LIMIT),
     )(pair_points.transpose(0, 2, 1, 3), pair_conf, live)
 
 
@@ -391,7 +408,7 @@
             pltpu.VMEM((terms, width), jnp.float32),
             pltpu.VMEM((terms, width), jnp.float32),
         ],
-        compiler_params=pltpu.CompilerParams(vmem_limit_bytes=VMEM_LIMIT),
+        compiler_params=pltpu.CompilerParams(vmem_limit_bytes=GRAD_VMEM_LIMIT),
     )(points, conf, wide, par, pair, pick, spread, cols, rows_)
 
 
@@ -418,21 +435,23 @@
     sem = pltpu.SemaphoreType.DMA((WIDTH,))
     turned = pltpu.VMEM((16 * rows, LANES), f32)
 
-    def call(kernel, ident, outs, scratch, *args):
+    def call(kernel, ident, outs, scratch, args, far):
         return pl.pallas_call(
             kernel,
             out_shape=outs,
-            in_specs=[VMEM] * len(args),
+            in_specs=[VMEM] * len(args) + [pl.BlockSpec(memory_space=pl.ANY)] * len(far),
             out_specs=[VMEM] * len(outs),
-            scratch_shapes=scratch,
+            scratch_shapes=scratch
+            + [pltpu.VMEM(a.shape, a.dtype) for a in far]
+            + [pltpu.SemaphoreType.DMA((len(far),))],
             compiler_params=pltpu.CompilerParams(
                 collective_id=ident, has_side_effects=True, vmem_limit_bytes=VMEM_LIMIT
             ),
-        )(*args)
+        )(*args, *far)
 
     wide, wide_par, served = call(
         functools.partial(first_kernel, n, rows, tiles), 0, wide_shape + [slot_shape],
-        [turned, message, message, sem, sem, sem, sem], wanted, log_depth, par,
+        [turned, message, message, sem, sem, sem, sem], (wanted, par), (log_depth,),
     )
 
     live = (jnp.arange(slots, dtype=jnp.int32) < pair_count[0]).astype(f32)
@@ -453,17 +472,18 @@
         grad_pair = tgrad[:, :7].reshape(slots, 2, 7).sum(axis=1).T
         count = adam_start + step_id + 1
         pair_params, pair_m, pair_v = adam_step(pair_params, grad_pair, pair_m, pair_v, count)
-        args = (grad, pgrad, served, log_depth, depth_m, depth_v, par, pmom, psec)
+        args = (pgrad, served, par, pmom, psec)
+        far = (grad, log_depth, depth_m, depth_v)
         if step_id < ITERS - 1:
             wide, wide_par, log_depth, depth_m, depth_v, par, pmom, psec = call(
                 functools.partial(middle_kernel, n, rows, tiles, count), 1 + step_id,
                 wide_shape + [big, big, big, small, small, small],
-                [turned, message, message, message, message, sem, sem, sem, sem], *args,
+                [turned, message, message, message, message, sem, sem, sem, sem], args, far,
             )
         else:
             log_depth, par = call(
                 functools.partial(last_kernel, n, rows, tiles, count), 1 + step_id, [big, small],
-                [turned, message, message, sem, sem], *args,
+                [turned, message, message, sem, sem], args, far,
             )
     return (log_depth, par[:, :7].T, pair_params)
 

time: 91.3 us -> 95.2 us (1.043)
  Pallas kernels: 69.4 us -> 78 us
  local copies, waits for them, and re-layouts: 19 us -> 14 us
    unnamed x34 -> x28, local copies, waits for them, and re-layouts: 17.7 us -> 12.6 us
    pallas_call x1, Pallas kernels: 3.97 us -> 8.05 us  [spread_pairs(): pl.pallas_call(spread_kernel, grid=(chunks,), in_specs=[pl.BlockSpec((slo...]
    pallas_call x2, Pallas kernels: 21.7 us -> 24.6 us  [term_grads(): pl.pallas_call(functools.partial(grad_kernel, chunks, pixels), grid=(chun...]
    pallas_call x3, Pallas kernels: 43.7 us -> 45.3 us  [call(): pl.pallas_call(kernel, out_shape=outs, in_specs=[VMEM] * len(args) + [pl....]
where the time goes in v2:
time: 95.2 us; the launch traced here: 94.2 us
  Pallas kernels  78 us (82%)
  local copies, waits for them, and re-layouts  14 us (15%)
  between operations  1.44 us (2%)
    pallas_call x3, Pallas kernels, call(): pl.pallas_call(kernel, out_shape=outs, in_specs=[VMEM] * len(args) + [pl....  45.3 us
    pallas_call x2, Pallas kernels, term_grads(): pl.pallas_call(functools.partial(grad_kernel, chunks, pixels), grid=(chun...  24.6 us
    unnamed x28, local copies, waits for them, and re-layouts  12.6 us
    pallas_call x1, Pallas kernels, spread_pairs(): pl.pallas_call(spread_kernel, grid=(chunks,), in_specs=[pl.BlockSpec((slo...  8.05 us

profile of v2, /device:TPU:0, one launch (start us, length us, event | category | flops | bytes accessed | tf_op | source)
XLA Modules:
  0.0 94.2 jit_solution(8809711002538622373)
XLA Ops:
  1.3 0.8 copy.41
  2.1 0.8 copy.44
  2.8 0.8 copy.45
  3.6 0.1 broadcast_in_dim.41
  3.7 0.1 broadcast_in_dim.42
  3.8 0.8 copy.43
  4.5 0.1 eq.30
  4.6 0.1 fusion.9.pick
  4.7 0.8 copy.50
  5.5 0.1 broadcast_in_dim.43.live
  5.6 0.7 broadcast_in_dim.45.wanted
  6.4 0.0 copy-start
  6.5 1.0 %copy-done = f32[8,12544]{1,0:T(8,128)S(1)} copy-done((f32[8,12544]{1,0:T(8,128)S(1)}, f32[8,12544]{1,0:T(8,128)}, u32[]{:S(2)}) %copy-start) | copy-done | bytes 401432
  7.4 18.9 %shard_map.158 = (f32[16,12544]{1,0:T(8,128)S(1)}, f32[16,128]{1,0:T(8,128)S(1)}, s32[9,8,128]{2,1,0:T(8,128)S(1)}) custom-call(s32[9,8,128]{2,1,0:T(8,128)S(1)} %broadcast_in_dim.45.wanted, f32[8,128]{1,0:T(8,128)S(1)} %pad.17.par, f32[8,12544]{1,0:T(8,128)S(1)} %copy-done), custom_call_target="tpu_custom_call" | custom-call | tf_op jit(solution)/shard_map/pallas_call | solution.py:439
  26.4 0.0 copy-start.2
  26.4 1.3 %copy-done.2 = bf16[24,2,12544]{2,1,0:T(2,128)(2,1)S(1)} copy-done((bf16[24,2,12544]{2,1,0:T(2,128)(2,1)S(1)}, bf16[24,2,12544]{2,1,0:T(2,128)(2,1)}, u32[]{:S(2)}) %copy-start.2) | copy-done | bytes 1204248
  27.7 8.0 %shard_map.157 = (f32[3,48,12544]{2,1,0:T(8,128)}, f32[48,12544]{1,0:T(8,128)S(1)}) custom-call(bf16[24,3,2,12544]{3,2,1,0:T(2,128)(2,1)} %bitcast.48, bf16[24,2,12544]{2,1,0:T(2,128)(2,1)S(1)} %copy-done.2, f32[48,128]{1,0:T(8,128)S(1)} %broadcast_in_dim.43.live), custom_call_target="tpu_custom_call" | custom-call | tf_op jit(solution)/shard_map/pallas_call | solution.py:364
  35.7 0.0 copy-start.7
  35.7 0.0 copy-start.8
  35.7 0.0 copy-start.9
  35.7 12.3 %shard_map.159 = (f32[16,12544]{1,0:T(8,128)S(1)}, f32[16,128]{1,0:T(8,128)S(1)}, f32[48,128]{1,0:T(8,128)S(1)}) custom-call(f32[3,48,12544]{2,1,0:T(8,128)} %get-tuple-element.24.pts, f32[48,12544]{1,0:T(8,128)S(1)} %get-tuple-element.25.conf, f32[16,12544]{1,0:T(8,128)S(1)} %get-tuple-element.26.wide, f32[16,128]{1,0:T(8,128)S(1)} %get-tuple-element.27.par, ...), custom_call_target="tpu_custom_call" | custom-call | tf_op jit(solution)/shard_map/pallas_call | solution.py:391
  48.1 0.0 copy-start.3
  48.1 0.9 copy-done.3
  49.0 0.1 copy.46
  49.1 0.0 copy-done.7
  49.1 0.0 copy-done.8
  49.1 0.0 copy-done.9
  49.1 0.1 copy.51
  49.2 0.0 copy-start.1
  49.2 1.0 %copy-done.1 = f32[8,12544]{1,0:T(8,128)S(1)} copy-done((f32[8,12544]{1,0:T(8,128)S(1)}, f32[8,12544]{1,0:T(8,128)}, u32[]{:S(2)}) %copy-start.1) | copy-done | bytes 401432
  50.2 0.0 copy-start.4
  50.2 1.1 %copy-done.4 = f32[16,12544]{1,0:T(8,128)S(1)} copy-done((f32[16,12544]{1,0:T(8,128)S(1)}, f32[16,12544]{1,0:T(8,128)}, u32[]{:S(2)}) %copy-start.4) | copy-done | bytes 802840
  51.4 0.0 copy-start.5
  51.4 1.0 %copy-done.5 = f32[8,12544]{1,0:T(8,128)S(1)} copy-done((f32[8,12544]{1,0:T(8,128)S(1)}, f32[8,12544]{1,0:T(8,128)}, u32[]{:S(2)}) %copy-start.5) | copy-done | bytes 401432
  52.4 0.0 copy-start.6
  52.4 1.0 %copy-done.6 = f32[8,12544]{1,0:T(8,128)S(1)} copy-done((f32[8,12544]{1,0:T(8,128)S(1)}, f32[8,12544]{1,0:T(8,128)}, u32[]{:S(2)}) %copy-start.6) | copy-done | bytes 401432
  53.4 15.8 %shard_map.160 = (f32[16,12544]{1,0:T(8,128)S(1)}, f32[16,128]{1,0:T(8,128)S(1)}, f32[8,12544]{1,0:T(8,128)S(1)}, f32[8,12544]{1,0:T(8,128)S(1)}, f32[8,12544]{1...) custom-call(f32[16,128]{1,0:T(8,128)S(1)} %get-tuple-element.28.pgrad, ...), custom_call_target="tpu_custom_call" | custom-call | tf_op jit(solution)/shard_map/pallas_call | solution.py:439
  69.2 12.3 %shard_map.161 = (f32[16,12544]{1,0:T(8,128)S(1)}, f32[16,128]{1,0:T(8,128)S(1)}, f32[48,128]{1,0:T(8,128)S(1)}) custom-call(f32[3,48,12544]{2,1,0:T(8,128)} %get-tuple-element.24.pts, f32[48,12544]{1,0:T(8,128)S(1)} %get-tuple-element.25.conf, f32[16,12544]{1,0:T(8,128)S(1)} %get-tuple-element.31.wide, f32[16,128]{1,0:T(8,128)S(1)} %get-tuple-element.32.par, ...), custom_call_target="tpu_custom_call" | custom-call | tf_op jit(solution)/shard_map/pallas_call | solution.py:391
  81.5 10.6 %shard_map.162 = (f32[8,12544]{1,0:T(8,128)S(1)}, f32[8,128]{1,0:T(8,128)S(1)}) custom-call(f32[16,128]{1,0:T(8,128)S(1)} %get-tuple-element.34.pgrad, s32[9,8,128]{2,1,0:T(8,128)S(1)} %get-tuple-element.29.served, f32[8,128]{1,0:T(8,128)S(1)} %get-tuple-element.35.par, f32[8,128]{1,0:T(8,128)S(1)} %get-tuple-element.36.pmom, ...), custom_call_target="tpu_custom_call" | custom-call | tf_op jit(solution)/shard_map/pallas_call | solution.py:439
  92.1 0.7 copy.49
  92.8 0.1 copy.48
  92.9 0.6 fusion.17
  93.5 0.7 copy.54
  (17 shorter events, 0.3 us)
Async XLA Ops:
  6.4 1.0 %copy-start = (f32[8,12544]{1,0:T(8,128)S(1)}, f32[8,12544]{1,0:T(8,128)}, u32[]{:S(2)}) copy-start(f32[8,12544]{1,0:T(8,128)} %depth_hbm.3) | copy-start | bytes 1204228
  26.4 1.3 %copy-start.2 = (bf16[24,2,12544]{2,1,0:T(2,128)(2,1)S(1)}, bf16[24,2,12544]{2,1,0:T(2,128)(2,1)}, u32[]{:S(2)}) copy-start(bf16[24,2,12544]{2,1,0:T(2,128)(2,1)} %raw_conf.1) | copy-start | bytes 3612676
  35.7 13.3 %copy-start.7 = (f32[7,24]{1,0:T(8,128)S(1)}, f32[7,24]{1,0:T(8,128)}, u32[]{:S(2)}) copy-start(f32[7,24]{1,0:T(8,128)} %param.22) | copy-start | bytes 2020
  35.7 13.4 %copy-start.8 = (f32[7,24]{1,0:T(8,128)S(1)}, f32[7,24]{1,0:T(8,128)}, u32[]{:S(2)}) copy-start(f32[7,24]{1,0:T(8,128)} %param.24) | copy-start | bytes 2020
  35.7 13.4 %copy-start.9 = (f32[7,24]{1,0:T(8,128)S(1)}, f32[7,24]{1,0:T(8,128)}, u32[]{:S(2)}) copy-start(f32[7,24]{1,0:T(8,128)} %param.23) | copy-start | bytes 2020
  48.1 0.9 copy-start.3
  49.2 1.0 %copy-start.1 = (f32[8,12544]{1,0:T(8,128)S(1)}, f32[8,12544]{1,0:T(8,128)}, u32[]{:S(2)}) copy-start(f32[8,12544]{1,0:T(8,128)} %depth_hbm.3) | copy-start | bytes 1204228
  50.2 1.1 %copy-start.4 = (f32[16,12544]{1,0:T(8,128)S(1)}, f32[16,12544]{1,0:T(8,128)}, u32[]{:S(2)}) copy-start(f32[16,12544]{1,0:T(8,128)} %copy-done.3) | copy-start | bytes 2408452
  51.4 1.0 %copy-start.5 = (f32[8,12544]{1,0:T(8,128)S(1)}, f32[8,12544]{1,0:T(8,128)}, u32[]{:S(2)}) copy-start(f32[8,12544]{1,0:T(8,128)} %mom_hbm.1) | copy-start | bytes 1204228
  52.4 1.0 %copy-start.6 = (f32[8,12544]{1,0:T(8,128)S(1)}, f32[8,12544]{1,0:T(8,128)}, u32[]{:S(2)}) copy-start(f32[8,12544]{1,0:T(8,128)} %sec_hbm.1) | copy-start | bytes 1204228
